TPU v7x, 128 devices: a whole 4x4x4 slice. The times are simulated.
128 devices in a mesh: dap: 64 (over z, y, x_hi, core), ch: 2 (over x_lo).
Axes of the slice: x: 4 (x_hi: 2, x_lo: 2; x = x_hi * 2 + x_lo), y: 4, z: 4, core: 2. Of those that a mesh axis runs over, the one named last changes fastest.
Arguments:
- pair: bfloat16 [256, 256, 128], P('dap'), may hold values from -6 to 6
- chain_lengths: int32 [4], replicated, may hold values from 32 to 64
- ln_gain: float32 [128], replicated, may hold values from 0.25 to 1.75
- ln_bias: float32 [128], replicated, may hold values from -3 to 3
- proj_weight: bfloat16 [4, 128, 128], P(None, None, 'ch'), may hold values from -0.5 to 0.5
- proj_bias: float32 [4, 128], P(None, 'ch'), may hold values from -3 to 3
- out_gain: float32 [128], P('ch'), may hold values from 0.25 to 1.75
- out_bias: float32 [128], P('ch'), may hold values from -3 to 3
- w_out: bfloat16 [128, 128], P('ch'), may hold values from -0.5 to 0.5
- out_shift: float32 [128], replicated, may hold values from -3 to 3
- w_gate: bfloat16 [128, 128], replicated, may hold values from -0.5 to 0.5
- gate_bias: float32 [128], replicated, may hold values from -3 to 3
- cotangent: bfloat16 [256, 256, 128], P('dap', 'ch'), may hold values from -6 to 6
Outputs:
- update: bfloat16 [256, 256, 128], P('dap', 'ch')
- pair_grad: bfloat16 [256, 256, 128], P('dap', 'ch')
Inputs may be any that keep to these rules, and one draw needn't show every extreme that they name: Chain m occupies residues m * 64 to (m + 1) * 64 - 1, of which the first chain_lengths[m] are real and the rest are padding.
All inputs are finite; a program needn't handle non-finite values.
Results may differ from a plain program's by a relative error of at most 0.012.
Values may be sent and summed in bfloat16 or wider, within the bound.
A program may use at most 64 MiB of HBM per device.

v0:
```python
import jax
import jax.numpy as jnp
from jax import lax
from jax.sharding import PartitionSpec as P

HID = 128
CHAINS = 4


epsilon = 1e-05


def copy_for_each(shard, axis):
    copies = jnp.broadcast_to(shard, (lax.axis_size(axis), *shard.shape))
    return lax.all_to_all(copies, axis, split_axis=0, concat_axis=0, tiled=True)


def taken_together(shard, axis):
    return copy_for_each(shard, axis).sum(axis=0)


def packed_total(arrays, axis):
    line, at, gathered = (jnp.concatenate([a.reshape(-1) for a in arrays]), 0, [])
    subtotal = taken_together(line, axis)
    for a in arrays:
        gathered.append(subtotal[at : at + a.size].reshape(a.shape))
        at += a.size
    return tuple(gathered)


def split_up(shard, dim, length):
    shape = shard.shape
    tiles = shard.reshape(*shape[:dim], length, shape[dim] // length, *shape[dim + 1 :])
    return jnp.moveaxis(tiles, dim, 0)


def sum_at_owner(shard, axis, dim):
    tiles = split_up(shard, dim, lax.axis_size(axis))
    arrived = lax.all_to_all(tiles, axis, split_axis=0, concat_axis=0, tiled=True)
    return arrived.astype(jnp.float32).sum(axis=0)


def in_order(tiles, dim):
    shape = list(tiles.shape[1:])
    shape[dim] *= tiles.shape[0]
    return jnp.moveaxis(tiles, 0, dim).reshape(shape)


def gathered_copies(shard, axis, dim):
    tiles = copy_for_each(shard, axis)
    return in_order(tiles, dim)


def layer_stats(values):
    mean = jnp.mean(values, axis=-1, keepdims=True)
    square = jnp.mean(values * values, axis=-1, keepdims=True)
    return (mean, lax.rsqrt(square - mean * mean + epsilon))


def per_device(
    pair,
    chain_lengths,
    ln_gain,
    ln_bias,
    proj_weight,
    proj_bias,
    out_gain,
    out_bias,
    w_out,
    out_shift,
    w_gate,
    gate_bias,
    cotangent,
):
    own_rows, residues, channels = pair.shape
    first_row = lax.axis_index("dap") * own_rows
    column_count = residues // lax.axis_size("ch")
    first_column = lax.axis_index("ch") * column_count
    slot_size = residues // CHAINS
    position = jnp.arange(residues, dtype=jnp.int32)
    owner = (position // slot_size)[:, None] == jnp.arange(CHAINS, dtype=jnp.int32)[None, :]
    chain_limit = jnp.sum(jnp.where(owner, chain_lengths[None, :], 0), axis=1)
    present = (position % slot_size < chain_limit).astype(jnp.float32)
    own_present = lax.dynamic_slice_in_dim(present, first_row, own_rows)
    pair_mask = own_present[:, None] * present[None, :]
    pair_float = pair.astype(jnp.float32)
    pair_mean, pair_scale = layer_stats(pair_float)
    pair_norm = (pair_float - pair_mean) * pair_scale
    normed = (pair_norm * ln_gain + ln_bias).astype(jnp.bfloat16)
    projected = (
        jnp.einsum("ijd,mdc->mcij", normed, proj_weight, preferred_element_type=jnp.float32)
        + proj_bias[:, :, None, None]
    )
    gate_left = jax.nn.sigmoid(projected[0])
    gate_right = jax.nn.sigmoid(projected[2])
    left_edge = (gate_left * projected[1] * pair_mask).astype(jnp.bfloat16)
    right_edge = (gate_right * projected[3] * pair_mask).astype(jnp.bfloat16)
    all_right = lax.all_gather(right_edge, "dap", axis=1, tiled=True)
    triangle = jnp.einsum("cik,cjk->cij", left_edge, all_right, preferred_element_type=jnp.float32)
    tri_sum, tri_square = packed_total(
        (jnp.sum(triangle, axis=0), jnp.sum(triangle * triangle, axis=0)), "ch"
    )
    tri_mean = tri_sum / HID
    tri_scale = lax.rsqrt(tri_square / HID - tri_mean * tri_mean + epsilon)
    tri_norm = (triangle - tri_mean) * tri_scale
    tri_out = (tri_norm * out_gain[:, None, None] + out_bias[:, None, None]).astype(jnp.bfloat16)
    out_terms = jnp.einsum("cij,cd->ijd", tri_out, w_out, preferred_element_type=jnp.float32)
    output_sum = sum_at_owner(out_terms.astype(jnp.bfloat16), "ch", 1) + out_shift
    normed_own = lax.dynamic_slice_in_dim(normed, first_column, column_count, 1)
    gate_value = jax.nn.sigmoid(
        jnp.einsum("ijd,de->ije", normed_own, w_gate, preferred_element_type=jnp.float32)
        + gate_bias
    )
    update = (gate_value * output_sum).astype(jnp.bfloat16)
    cot_float = cotangent.astype(jnp.float32)
    grad_out = (cot_float * gate_value).astype(jnp.bfloat16)
    grad_gate = (cot_float * output_sum * gate_value * (1.0 - gate_value)).astype(jnp.bfloat16)
    grad_full = gathered_copies(grad_out, "ch", 1)
    grad_normed = jnp.einsum("ijd,cd->cij", grad_full, w_out, preferred_element_type=jnp.float32)
    grad_scaled = grad_normed * out_gain[:, None, None]
    scaled_sum, scaled_cross = packed_total(
        (jnp.sum(grad_scaled, axis=0), jnp.sum(grad_scaled * tri_norm, axis=0)), "ch"
    )
    grad_tri = (
        tri_scale * (grad_scaled - scaled_sum / HID - tri_norm * scaled_cross / HID)
    ).astype(jnp.bfloat16)
    grad_left = jnp.einsum("cij,cjk->cik", grad_tri, all_right, preferred_element_type=jnp.float32)
    swapped = lax.all_to_all(grad_tri, "dap", split_axis=2, concat_axis=1, tiled=True)
    grad_right = jnp.einsum(
        "cij,cik->cjk",
        swapped,
        lax.all_gather(left_edge, "dap", axis=1, tiled=True),
        preferred_element_type=jnp.float32,
    )
    grad_proj = jnp.stack(
        [
            (grad_left * projected[1] * pair_mask * gate_left * (1.0 - gate_left)).astype(
                jnp.bfloat16
            ),
            (grad_left * gate_left * pair_mask).astype(jnp.bfloat16),
            (grad_right * projected[3] * pair_mask * gate_right * (1.0 - gate_right)).astype(
                jnp.bfloat16
            ),
            (grad_right * gate_right * pair_mask).astype(jnp.bfloat16),
        ]
    )
    proj_terms = jnp.einsum(
        "mcij,mdc->ijd", grad_proj, proj_weight, preferred_element_type=jnp.float32
    )
    grad_pair = sum_at_owner(proj_terms.astype(jnp.bfloat16), "ch", 1)
    grad_pair = grad_pair + jnp.einsum(
        "ije,de->ijd", grad_gate, w_gate, preferred_element_type=jnp.float32
    )
    pair_scaled = grad_pair * ln_gain
    norm_own = lax.dynamic_slice_in_dim(pair_norm, first_column, column_count, 1)
    scale_own = lax.dynamic_slice_in_dim(pair_scale, first_column, column_count, 1)
    own_grad = (
        scale_own
        * (
            pair_scaled
            - jnp.mean(pair_scaled, axis=-1, keepdims=True)
            - norm_own * jnp.mean(pair_scaled * norm_own, axis=-1, keepdims=True)
        )
    ).astype(jnp.bfloat16)
    return (update, own_grad)


def solution(mesh):
    placed = (
        P("dap", None, None),
        P(),
        P(),
        P(),
        P(None, None, "ch"),
        P(None, "ch"),
        P("ch"),
        P("ch"),
        P("ch", None),
        P(),
        P(),
        P(),
        P("dap", "ch", None),
    )
    return jax.shard_map(
        per_device,
        mesh=mesh,
        in_specs=placed,
        out_specs=(P("dap", "ch", None), P("dap", "ch", None)),
        check_vma=False,
    )
```

profile of v0, /device:TPU:1, one launch (start us, length us, event | category | flops | bytes accessed | tf_op | source)
XLA Modules:
  0.0 208.2 jit_solution(6382815073767069801)
XLA Ops:
  7.2 0.0 copy-start
  7.2 0.0 copy-start.7
  7.2 0.0 copy-start.5
  7.2 0.0 copy-start.2
  7.2 0.0 copy-start.1
  7.2 0.0 copy-start.6
  7.3 0.0 all-gather.3.cloned.1.call-start
  7.3 1.3 convert_reduce_fusion
  8.6 0.7 select_reduce_fusion
  9.3 0.1 dynamic_slice.13
  9.4 0.1 broadcast_multiply_fusion
  9.5 1.3 fusion.14
  10.8 0.0 copy-done
  10.8 1.0 fusion.6
  11.8 0.8 multiply_convert_fusion.8
  12.7 0.0 all-gather.3.cloned.1.call-update
  12.7 0.0 all-gather.5.cloned.1.call-start
  12.7 0.7 all-gather.5.cloned.1.call-update
  13.4 84.6 %all-gather.3.cloned.1.call-done = bf16[64,256,256]{2,0,1:T(8,128)(2,1)} async-done(((bf16[64,4,256]{2,0,1:T(8,128)(2,1)}), bf16[64,256,256]{2,0,1:T(8,128)(2,1)}) %all-gather.3.cloned.1.call-update) | async-done | bytes 8388624 | tf_op jit(solution)/shard_map/all_gather | solution.py:98
  98.1 8.0 %fusion.65 = (f32[4,256]{1,0:T(4,128)S(1)}, f32[4,256]{1,0:T(4,128)S(1)}, f32[64,4,256]{2,1,0:T(4,128)S(1)}) fusion(bf16[64,256,256]{2,0,1:T(8,128)(2,1)} %all-gather.3.cloned.1.call-done, bf16[64,4,256]{2,0,1:T(8,128)(2,1)} %get-tuple-element.16), kind=kOutput, calls=%fused_computation.118 | convolution fusion | flops 33748992 | bytes 8790016 | tf_op jit(solution)/shard_map/cik,cjk->cij/dot_general | solution.py:99
  106.1 5.1 %all_to_all.45 = f32[2,1,2048]{2,1,0:T(1,128)S(1)} all-to-all(f32[2,1,2048]{2,1,0:T(1,128)S(1)} %broadcast_in_dim.20), channel_id=1, replica_groups=mesh['dap'=64,'ch'=2] {'ch'}, dimensions={0} | all-to-all | bytes 32768 | tf_op jit(solution)/shard_map/all_to_all | solution.py:15
  111.3 0.3 convolution_convert_fusion
  111.7 0.7 copy.213
  112.4 3.4 %all-to-all-start.1 = ((bf16[2,4,128,128]{3,2,1,0:T(8,128)(2,1)}), bf16[2,4,128,128]{3,2,1,0:T(8,128)(2,1)S(1)}, u32[]{:S(2)}, u32[]{:S(2)}) async-start(bf16[2,4,128,128]{3,2,1,0:T(8,128)(2,1)} %bitcast.139), calls=%async_computation.1 | async-start | bytes 524288 | tf_op jit(solution)/shard_map/all_to_all | solution.py:39
  115.8 4.4 %all-to-all-done.1 = bf16[2,4,128,128]{3,2,1,0:T(8,128)(2,1)S(1)} async-done(((bf16[2,4,128,128]{3,2,1,0:T(8,128)(2,1)}), bf16[2,4,128,128]{3,2,1,0:T(8,128)(2,1)S(1)}, u32[]{:S(2)}, u32[]{:S(2)}) %all-to-all-start.1) | async-done | bytes 262176 | tf_op jit(solution)/shard_map/all_to_all | solution.py:39
  120.3 0.9 fusion.23
  121.3 6.4 %all_to_all.46 = bf16[2,4,128,128]{3,2,1,0:T(8,128)(2,1)S(1)} all-to-all(bf16[2,4,128,128]{3,2,1,0:T(8,128)(2,1)S(1)} %broadcast_in_dim.21), channel_id=1, replica_groups=mesh['dap'=64,'ch'=2] {'ch'}, dimensions={0} | all-to-all | bytes 524288 | tf_op jit(solution)/shard_map/all_to_all | solution.py:15
  127.7 0.2 fusion.64
  128.0 5.1 %all_to_all.47 = f32[2,1,2048]{2,1,0:T(1,128)S(1)} all-to-all(f32[2,1,2048]{2,1,0:T(1,128)S(1)} %broadcast_in_dim.22), channel_id=1, replica_groups=mesh['dap'=64,'ch'=2] {'ch'}, dimensions={0} | all-to-all | bytes 32768 | tf_op jit(solution)/shard_map/all_to_all | solution.py:15
  133.1 0.1 multiply_convert_fusion.5
  133.2 0.2 copy.149
  133.4 0.8 reshape.215
  134.2 12.1 %all-to-all-start.4 = ((bf16[64,2,512]{2,1,0:T(2,128)(2,1)}), bf16[64,2,512]{2,1,0:T(2,128)(2,1)S(1)}, u32[]{:S(2)}, u32[]{:S(2)}) async-start(bf16[64,2,512]{2,1,0:T(2,128)(2,1)} %reshape.215), calls=%async_computation.4 | async-start | bytes 262144 | tf_op jit(solution)/shard_map/all_to_all | solution.py:128
  146.3 7.9 %fusion.2 = f32[64,4,256]{2,1,0:T(4,128)S(1)} fusion(bf16[64,256,256]{2,0,1:T(8,128)(2,1)} %all-gather.3.cloned.1.call-done, bf16[64,4,256]{2,0,1:T(8,128)(2,1)S(1)} %multiply_convert_fusion.5), kind=kOutput, calls=%fused_computation.2 | convolution fusion | flops 33554432 | bytes 8781824 | tf_op jit(solution)/shard_map/cij,cjk->cik/dot_general | solution.py:127
  154.2 2.1 %all-to-all-done.4 = bf16[64,2,512]{2,1,0:T(2,128)(2,1)S(1)} async-done(((bf16[64,2,512]{2,1,0:T(2,128)(2,1)}), bf16[64,2,512]{2,1,0:T(2,128)(2,1)S(1)}, u32[]{:S(2)}, u32[]{:S(2)}) %all-to-all-start.4) | async-done | bytes 131104 | tf_op jit(solution)/shard_map/all_to_all | solution.py:128
  156.3 0.2 reshape.216
  156.6 0.2 copy.151
  156.8 0.2 copy.152
  157.0 25.3 %all-gather.5.cloned.1.call-done = bf16[64,256,256]{2,0,1:T(8,128)(2,1)} async-done(((bf16[64,4,256]{2,0,1:T(8,128)(2,1)}), bf16[64,256,256]{2,0,1:T(8,128)(2,1)}) %all-gather.5.cloned.1.call-update) | async-done | bytes 8388624 | tf_op jit(solution)/shard_map/all_gather | solution.py:132
  182.3 7.9 %fusion = f32[64,4,256]{2,1,0:T(4,128)S(1)} fusion(bf16[64,256,4]{1,2,0:T(4,128)(2,1)S(1)} %copy.152, bf16[64,256,256]{2,0,1:T(8,128)(2,1)} %all-gather.5.cloned.1.call-done), kind=kOutput, calls=%fused_computation | convolution fusion | flops 33554432 | bytes 8781824 | tf_op jit(solution)/shard_map/cij,cik->cjk/dot_general | solution.py:129
  190.2 0.3 fusion.39
  190.5 0.4 fusion.7
  190.8 0.7 copy.212
  191.5 3.4 %all-to-all-start.5 = ((bf16[2,4,128,128]{3,2,1,0:T(8,128)(2,1)}), bf16[2,4,128,128]{3,2,1,0:T(8,128)(2,1)S(1)}, u32[]{:S(2)}, u32[]{:S(2)}) async-start(bf16[2,4,128,128]{3,2,1,0:T(8,128)(2,1)} %bitcast.138), calls=%async_computation.5 | async-start | bytes 524288 | tf_op jit(solution)/shard_map/all_to_all | solution.py:39
  195.0 5.0 %all-to-all-done.5 = bf16[2,4,128,128]{3,2,1,0:T(8,128)(2,1)S(1)} async-done(((bf16[2,4,128,128]{3,2,1,0:T(8,128)(2,1)}), bf16[2,4,128,128]{3,2,1,0:T(8,128)(2,1)S(1)}, u32[]{:S(2)}, u32[]{:S(2)}) %all-to-all-start.5) | async-done | bytes 262176 | tf_op jit(solution)/shard_map/all_to_all | solution.py:39
  200.0 0.0 copy-done.4
  200.1 0.4 fusion.63
  200.5 0.9 multiply_convert_fusion
  (37 shorter events, 0.4 us)
Async XLA Ops:
  7.2 3.7 %copy-start = (bf16[4,128,64]{1,2,0:T(8,128)(2,1)S(1)}, bf16[4,128,64]{1,2,0:T(8,128)(2,1)}, u32[]{:S(2)}) copy-start(bf16[4,128,64]{1,2,0:T(8,128)(2,1)} %param.17) | copy-start | bytes 196612
  7.2 104.1 %copy-start.7 = (f32[64]{0:T(128)S(1)}, f32[64]{0:T(128)}, u32[]{:S(2)}) copy-start(f32[64]{0:T(128)} %param.20) | copy-start | bytes 772
  7.2 104.1 %copy-start.5 = (f32[64]{0:T(128)S(1)}, f32[64]{0:T(128)}, u32[]{:S(2)}) copy-start(f32[64]{0:T(128)} %param.19) | copy-start | bytes 772
  7.2 104.1 %copy-start.2 = (bf16[64,128]{1,0:T(8,128)(2,1)S(1)}, bf16[64,128]{1,0:T(8,128)(2,1)}, u32[]{:S(2)}) copy-start(bf16[64,128]{1,0:T(8,128)(2,1)} %param.21) | copy-start | bytes 49156
  7.2 113.1 %copy-start.1 = (bf16[4,128,128]{2,1,0:T(8,128)(2,1)S(1)}, bf16[4,128,128]{2,1,0:T(8,128)(2,1)}, u32[]{:S(2)}) copy-start(bf16[4,128,128]{2,1,0:T(8,128)(2,1)} %param.25) | copy-start | bytes 393220
  7.2 113.1 %copy-start.6 = (f32[128]{0:T(128)S(1)}, f32[128]{0:T(128)}, u32[]{:S(2)}) copy-start(f32[128]{0:T(128)} %param.22) | copy-start | bytes 1540
  7.2 113.1 %copy-start.8 = (f32[128]{0:T(128)S(1)}, f32[128]{0:T(128)}, u32[]{:S(2)}) copy-start(f32[128]{0:T(128)} %param.24) | copy-start | bytes 1540
  7.2 113.1 %copy-start.3 = (bf16[128,128]{1,0:T(8,128)(2,1)S(1)}, bf16[128,128]{1,0:T(8,128)(2,1)}, u32[]{:S(2)}) copy-start(bf16[128,128]{1,0:T(8,128)(2,1)} %param.23) | copy-start | bytes 98308
  7.3 90.8 %all-gather.3.cloned.1.call-start = ((), (), s32[]{:S(2)}) async-start(), calls=%async_computation.6 | async-start | bytes 8519680 | tf_op jit(solution)/shard_map/all_gather | solution.py:98
  12.7 169.6 %all-gather.5.cloned.1.call-start = ((), (), s32[]{:S(2)}) async-start(), calls=%async_computation.7 | async-start | bytes 8519680 | tf_op jit(solution)/shard_map/all_gather | solution.py:132
  112.4 7.9 %all-to-all-start.1 = ((bf16[2,4,128,128]{3,2,1,0:T(8,128)(2,1)}), bf16[2,4,128,128]{3,2,1,0:T(8,128)(2,1)S(1)}, u32[]{:S(2)}, u32[]{:S(2)}) async-start(bf16[2,4,128,128]{3,2,1,0:T(8,128)(2,1)} %bitcast.139), calls=%async_computation.1 | async-start | bytes 524288 | tf_op jit(solution)/shard_map/all_to_all | solution.py:39
  134.2 22.1 %all-to-all-start.4 = ((bf16[64,2,512]{2,1,0:T(2,128)(2,1)}), bf16[64,2,512]{2,1,0:T(2,128)(2,1)S(1)}, u32[]{:S(2)}, u32[]{:S(2)}) async-start(bf16[64,2,512]{2,1,0:T(2,128)(2,1)} %reshape.215), calls=%async_computation.4 | async-start | bytes 262144 | tf_op jit(solution)/shard_map/all_to_all | solution.py:128
  154.2 45.8 %copy-start.4 = (f32[128]{0:T(128)S(1)}, f32[128]{0:T(128)}, u32[]{:S(2)}) copy-start(f32[128]{0:T(128)} %param.15) | copy-start | bytes 1540
  191.5 8.5 %all-to-all-start.5 = ((bf16[2,4,128,128]{3,2,1,0:T(8,128)(2,1)}), bf16[2,4,128,128]{3,2,1,0:T(8,128)(2,1)S(1)}, u32[]{:S(2)}, u32[]{:S(2)}) async-start(bf16[2,4,128,128]{3,2,1,0:T(8,128)(2,1)} %bitcast.138), calls=%async_computation.5 | async-start | bytes 524288 | tf_op jit(solution)/shard_map/all_to_all | solution.py:39
Sparse Core Ops, SparseCore 0:
  12.8 85.2 all-gather.2
  101.7 80.5 all-gather.4
where the time goes:
time: 209 us; the launch traced here: 208 us
  waiting for transfers between devices  122 us (58%)
  matrix products  27 us (13%)
  starting transfers between devices  19.1 us (9%)
  blocking collectives  16.5 us (8%)
  between operations  14.4 us (7%)
  other arithmetic  5.7 us (3%)
  local copies, waits for them, and re-layouts  3.3 us (2%)
    all_gather x1, waiting for transfers between devices, per_device(): all_right = lax.all_gather(right_edge, 'dap', axis=1, tiled=True)  84.6 us
    all_gather x1, waiting for transfers between devices, per_device(): lax.all_gather(left_edge, 'dap', axis=1, tiled=True)  25.3 us
    all_to_all x3, blocking collectives, copy_for_each(): return lax.all_to_all(copies, axis, split_axis=0, concat_axis=0, tiled=True)  16.5 us
    all_to_all x1, starting transfers between devices, per_device(): lax.all_to_all(grad_tri, 'dap', split_axis=2, concat_axis=1, tiled=True)  12.1 us
    all_to_all x2, waiting for transfers between devices, sum_at_owner(): lax.all_to_all(tiles, axis, split_axis=0, concat_axis=0, tiled=True)  9.42 us
    dot_general x1, matrix products, per_device(): jnp.einsum('cik,cjk->cij', left_edge, all_right, preferred_element_type=j...  8.04 us
    dot_general x1, matrix products, per_device(): jnp.einsum('cij,cjk->cik', grad_tri, all_right, preferred_element_type=jn...  7.92 us
    dot_general x1, matrix products, per_device(): jnp.einsum('cij,cik->cjk', swapped, lax.all_gather(left_edge, 'dap', axis...  7.88 us
  transfers between devices with their start and end apart: 5, of which 5 were waited for; matrix products, arithmetic and copies ran while one was open for 10% of the time, Pallas kernels for 0%

commit v1 on v0

v1 whole, which is shorter than its diff:
```python
import jax
import jax.numpy as jnp
from jax import lax
from jax.experimental import pallas as pl
from jax.experimental.pallas import tpu as pltpu
from jax.sharding import PartitionSpec as P

EPS = 1e-05
F32 = jnp.float32
BF16 = jnp.bfloat16
MESH = pl.DeviceIdType.MESH


def sigmoid(x):
    return 0.5 * jnp.tanh(0.5 * x) + 0.5


def mm(a, b):
    return lax.dot_general(a, b, (((1,), (0,)), ((), ())), preferred_element_type=F32)


def mm_nt(a, b):
    return lax.dot_general(a, b, (((1,), (1,)), ((), ())), preferred_element_type=F32)


def mm_tn(a, b):
    return lax.dot_general(a, b, (((0,), (0,)), ((), ())), preferred_element_type=F32)


def column(block, n, rows):
    return jnp.broadcast_to(block[0:rows, n : n + 1], (rows, 128))


def mean0(x):
    return jnp.sum(x, axis=0, keepdims=True) * (1.0 / 128.0)


def kernel(
    pair,
    lens,
    ln_gain,
    ln_bias,
    pw,
    pb,
    out_gain,
    out_bias,
    w_out,
    out_shift,
    w_gate,
    gate_bias,
    cot,
    update,
    pair_grad,
    wt,
    wo,
    hv,
    vec,
    pnorm,
    pscale,
    normed,
    s1f,
    s1,
    r1,
    r1f,
    lmat,
    rmat,
    s2,
    r2,
    s3,
    r3,
    gmat,
    s4f,
    s4,
    r4,
    r4f,
    factor,
    gate_t,
    cot_t,
    gs_t,
    m1_t,
    tn_t,
    part_t,
    wo_t,
    back_w,
    gp,
    wsem_s,
    wsem_r,
    ssem,
    rsem,
):
    p = lax.axis_index("dap")
    g = lax.axis_index("ch")
    me = g * 64 + p

    barrier = pltpu.get_barrier_semaphore()

    def greet(k, carry):
        t = lax.rem(me + k, 128)
        pl.semaphore_signal(
            barrier, inc=1, device_id=(lax.rem(t, 64), t // 64), device_id_type=MESH
        )
        return carry

    lax.fori_loop(1, 128, greet, 0)

    for m in range(4):
        wt[g, m * 64 : (m + 1) * 64, :] = pw[m].T
    wo[g] = w_out[...]
    hv[g] = jnp.zeros((8, 128), F32)
    hv[g, 0:4, 0:64] = pb[...]
    hv[g, 4:5, 0:64] = out_gain[...]
    hv[g, 5:6, 0:64] = out_bias[...]
    vec[...] = jnp.zeros((8, 128), F32)
    vec[0:1, :] = ln_gain[...]
    vec[1:2, :] = ln_bias[...]
    vec[2:3, :] = out_shift[...]
    vec[3:4, :] = gate_bias[...]
    vcol = vec[...].T
    gain_c = column(vcol, 0, 128)
    bias_c = column(vcol, 1, 128)
    hcol = hv[g].T
    proj_c = [column(hcol, m, 64) for m in range(4)]

    lane = lax.broadcasted_iota(jnp.int32, (1, 128), 1)
    low = lane < 64
    slot = jnp.where(low, lane, lane - 64)

    def present_columns(first_chain):
        limit = jnp.where(low, lens[first_chain], lens[first_chain + 1])
        return jnp.where(slot < limit, 1.0, 0.0)

    row_limit = jnp.full((1, 128), lens[p // 16], jnp.int32)
    row_present = [
        jnp.where(row_limit > lax.rem(p * 4 + i, 64), 1.0, 0.0) for i in range(4)
    ]

    columns = [present_columns(0), present_columns(2)]
    for i in range(4):
        for kh in range(2):
            t = i * 2 + kh
            x = pair[i, kh * 128 : (kh + 1) * 128, :].T.astype(F32)
            mean = mean0(x)
            scale = lax.rsqrt(mean0(x * x) - mean * mean + EPS)
            norm = (x - mean) * scale
            pnorm[t] = norm
            pscale[t] = scale
            nb = (norm * gain_c + bias_c).astype(BF16)
            normed[t] = nb
            mask = row_present[i] * columns[kh]
            pr = mm(wt[g], nb)
            left = sigmoid(pr[0:64] + proj_c[0]) * (pr[64:128] + proj_c[1]) * mask
            right = sigmoid(pr[128:192] + proj_c[2]) * (pr[192:256] + proj_c[3]) * mask
            s1f[pl.ds(i * 4 + kh, 64, stride=16), :] = left
            s1f[pl.ds(i * 4 + 2 + kh, 64, stride=16), :] = right
    s1[...] = s1f[...].reshape(64, 16, 128).astype(BF16)

    pl.semaphore_wait(barrier, 127)

    own1 = pltpu.make_async_copy(s1.at[p], r1.at[p], rsem.at[0])
    own1.start()

    def send1(k, carry):
        t = lax.rem(p + k, 64)
        pltpu.make_async_remote_copy(
            src_ref=s1.at[t],
            dst_ref=r1.at[p],
            send_sem=ssem.at[0],
            recv_sem=rsem.at[0],
            device_id=(t, g),
            device_id_type=MESH,
        ).start()
        return carry

    lax.fori_loop(1, 64, send1, 0)

    swaps = [
        pltpu.make_async_remote_copy(
            src_ref=ref.at[g],
            dst_ref=ref.at[g],
            send_sem=wsem_s.at[n],
            recv_sem=wsem_r.at[n],
            device_id=(p, 1 - g),
            device_id_type=MESH,
        )
        for n, ref in enumerate((wt, wo, hv))
    ]
    for swap in swaps:
        swap.start()

    gate_w = w_gate[...].T
    gate_c = column(vcol, 3, 128)
    own_columns = present_columns(g * 2)
    for i in range(4):
        gate = sigmoid(mm(gate_w, normed[i * 2 + g]) + gate_c)
        gate_t[i] = gate
        cot_t[i] = cot[i].T.astype(F32)
    for swap in swaps:
        swap.wait()
    halves = [hv[0].T, hv[1].T]
    full = [
        jnp.concatenate([column(halves[0], n, 64), column(halves[1], n, 64)], axis=0)
        for n in (4, 5)
    ]
    wo_full = wo[...].reshape(128, 128)
    for i in range(4):
        grad_out = (cot_t[i] * gate_t[i]).astype(BF16)
        gs = mm(wo_full, grad_out) * full[0]
        gs_t[i] = gs
        m1_t[i] = mean0(gs)
    wo_t[...] = wo_full.T
    back_w[...] = wt[...].reshape(512, 128).astype(F32).T.astype(BF16)

    for h in range(2):
        bias = [column(halves[h], m, 64) for m in range(4)]
        rows = slice(h * 64, (h + 1) * 64)
        for i in range(4):
            pr = mm(wt[h], normed[i * 2 + g])
            mask = row_present[i] * own_columns
            for side in range(2):
                n = side * 2
                s = sigmoid(pr[n * 64 : n * 64 + 64] + bias[n])
                sm = s * mask
                value = pr[n * 64 + 64 : n * 64 + 128] + bias[n + 1]
                factor[i, n, rows, :] = value * sm * (1.0 - s)
                factor[i, n + 1, rows, :] = sm

    pltpu.make_async_copy(r1, r1, rsem.at[0]).wait()
    r1f[...] = r1[...].reshape(1024, 128).astype(F32)
    for kh in range(2):
        cols = slice(kh * 128, (kh + 1) * 128)
        lmat[:, cols] = r1f[pl.ds(kh, 256, stride=4), :].astype(BF16)
        rmat[:, cols] = r1f[pl.ds(2 + kh, 256, stride=4), :].astype(BF16)
    for h in range(2):
        s2[h * 256 : (h + 1) * 256, :] = mm_nt(
            lmat[...], rmat[h * 128 : (h + 1) * 128, :]
        )

    def spread(source, target, n):
        mine = pl.ds(pl.multiple_of(me * 4, 4), 4)
        pltpu.make_async_copy(source.at[mine], target.at[mine], rsem.at[n]).start()

        def send(k, carry):
            t = lax.rem(me + k, 128)
            pltpu.make_async_remote_copy(
                src_ref=source.at[pl.ds(pl.multiple_of(t * 4, 4), 4)],
                dst_ref=target.at[mine],
                send_sem=ssem.at[n],
                recv_sem=rsem.at[n],
                device_id=(lax.rem(t, 64), t // 64),
                device_id_type=MESH,
            ).start()
            return carry

        lax.fori_loop(1, 128, send, 0)

    spread(s2, r2, 1)
    pltpu.make_async_copy(r2, r2, rsem.at[1]).wait()

    for i in range(4):
        tri = r2[pl.ds(i, 128, stride=4), :]
        mean = mean0(tri)
        scale = lax.rsqrt(mean0(tri * tri) - mean * mean + EPS)
        tn = (tri - mean) * scale
        tn_t[i] = tn
        gs = gs_t[i]
        grad = scale * (gs - m1_t[i] - tn * mean0(gs * tn))
        s3[pl.ds(i, 128, stride=4), :] = grad
    spread(s3, r3, 2)

    shift_c = column(vcol, 2, 128)
    for i in range(4):
        tri_out = (tn_t[i] * full[0] + full[1]).astype(BF16)
        out_sum = mm(wo_t[...], tri_out) + shift_c
        gate = gate_t[i]
        gated = gate * out_sum
        update[i] = gated.T.astype(BF16)
        grad_gate = (cot_t[i] * gated * (1.0 - gate)).astype(BF16)
        part_t[i] = mm(w_gate[...], grad_gate)

    pltpu.make_async_copy(r3, r3, rsem.at[2]).wait()
    for h in range(2):
        gmat[:, h * 128 : (h + 1) * 128] = r3[h * 256 : (h + 1) * 256, :].astype(BF16)
    grads = (mm(gmat[...], rmat[...]), mm_tn(gmat[...], lmat[...]))
    for side in range(2):
        for h in range(2):
            s4f[pl.ds(h * 512 + side, 256, stride=2), :] = grads[side][
                :, h * 128 : (h + 1) * 128
            ]
    s4[...] = s4f[...].reshape(128, 8, 128).astype(BF16)
    pltpu.make_async_copy(s4.at[me], r4.at[me], rsem.at[3]).start()

    def send4(k, carry):
        t = lax.rem(me + k, 128)
        pltpu.make_async_remote_copy(
            src_ref=s4.at[t],
            dst_ref=r4.at[me],
            send_sem=ssem.at[3],
            recv_sem=rsem.at[3],
            device_id=(lax.rem(t, 64), t // 64),
            device_id_type=MESH,
        ).start()
        return carry

    lax.fori_loop(1, 128, send4, 0)
    pltpu.make_async_copy(r4, r4, rsem.at[3]).wait()

    r4f[...] = r4[...].astype(F32).reshape(1024, 128)
    for i in range(4):
        for side in range(2):
            edge = r4f[pl.ds(i * 2 + side, 128, stride=8), :]
            for n in range(2):
                m = side * 2 + n
                prod = (edge * factor[i, m]).astype(BF16)
                for h in range(2):
                    at = h * 256 + m * 64
                    gp[at : at + 64, i * 128 : (i + 1) * 128] = prod[
                        h * 64 : (h + 1) * 64
                    ]
    for i in range(4):
        grad = mm(back_w[...], gp[:, i * 128 : (i + 1) * 128]) + part_t[i]
        ps = grad * gain_c
        norm = pnorm[i * 2 + g]
        own = pscale[i * 2 + g] * (ps - mean0(ps) - norm * mean0(ps * norm))
        pair_grad[i] = own.T.astype(BF16)

    blocks = s1.at[pl.ds(0, 63)]
    pltpu.make_async_copy(blocks, blocks, ssem.at[0]).wait()
    for n, ref in ((1, s2), (2, s3)):
        blocks = ref.at[pl.ds(0, 508)]
        pltpu.make_async_copy(blocks, blocks, ssem.at[n]).wait()
    blocks = s4.at[pl.ds(0, 127)]
    pltpu.make_async_copy(blocks, blocks, ssem.at[3]).wait()


def per_device(
    pair,
    chain_lengths,
    ln_gain,
    ln_bias,
    proj_weight,
    proj_bias,
    out_gain,
    out_bias,
    w_out,
    out_shift,
    w_gate,
    gate_bias,
    cotangent,
):
    def row(v):
        return v.reshape(1, -1)

    vmem = pl.BlockSpec(memory_space=pltpu.VMEM)
    smem = pl.BlockSpec(memory_space=pltpu.SMEM)
    out = jax.ShapeDtypeStruct((4, 128, 128), BF16)
    return pl.pallas_call(
        kernel,
        out_shape=(out, out),
        in_specs=[vmem, smem] + [vmem] * 11,
        out_specs=(vmem, vmem),
        scratch_shapes=[
            pltpu.VMEM((2, 256, 128), BF16),
            pltpu.VMEM((2, 64, 128), BF16),
            pltpu.VMEM((2, 8, 128), F32),
            pltpu.VMEM((8, 128), F32),
            pltpu.VMEM((8, 128, 128), F32),
            pltpu.VMEM((8, 1, 128), F32),
            pltpu.VMEM((8, 128, 128), BF16),
            pltpu.VMEM((1024, 128), F32),
            pltpu.VMEM((64, 16, 128), BF16),
            pltpu.VMEM((64, 16, 128), BF16),
            pltpu.VMEM((1024, 128), F32),
            pltpu.VMEM((256, 256), BF16),
            pltpu.VMEM((256, 256), BF16),
            pltpu.VMEM((512, 128), F32),
            pltpu.VMEM((512, 128), F32),
            pltpu.VMEM((512, 128), F32),
            pltpu.VMEM((512, 128), F32),
            pltpu.VMEM((256, 256), BF16),
            pltpu.VMEM((1024, 128), F32),
            pltpu.VMEM((128, 8, 128), BF16),
            pltpu.VMEM((128, 8, 128), BF16),
            pltpu.VMEM((1024, 128), F32),
            pltpu.VMEM((4, 4, 128, 128), F32),
            pltpu.VMEM((4, 128, 128), F32),
            pltpu.VMEM((4, 128, 128), F32),
            pltpu.VMEM((4, 128, 128), F32),
            pltpu.VMEM((4, 1, 128), F32),
            pltpu.VMEM((4, 128, 128), F32),
            pltpu.VMEM((4, 128, 128), F32),
            pltpu.VMEM((128, 128), BF16),
            pltpu.VMEM((128, 512), BF16),
            pltpu.VMEM((512, 512), BF16),
            pltpu.SemaphoreType.DMA((3,)),
            pltpu.SemaphoreType.DMA((3,)),
            pltpu.SemaphoreType.DMA((4,)),
            pltpu.SemaphoreType.DMA((4,)),
        ],
        compiler_params=pltpu.CompilerParams(
            collective_id=0, has_side_effects=True, vmem_limit_bytes=40 << 20
        ),
    )(
        pair,
        chain_lengths,
        row(ln_gain),
        row(ln_bias),
        proj_weight,
        proj_bias,
        row(out_gain),
        row(out_bias),
        w_out,
        row(out_shift),
        w_gate,
        row(gate_bias),
        cotangent,
    )


def solution(mesh):
    placed = (
        P("dap", None, None),
        P(),
        P(),
        P(),
        P(None, None, "ch"),
        P(None, "ch"),
        P("ch"),
        P("ch"),
        P("ch", None),
        P(),
        P(),
        P(),
        P("dap", "ch", None),
    )
    return jax.shard_map(
        per_device,
        mesh=mesh,
        in_specs=placed,
        out_specs=(P("dap", "ch", None), P("dap", "ch", None)),
        check_vma=False,
    )
```

time: 209 us -> 49.7 us (0.24)
  waiting for transfers between devices: 122 us -> 0 us
  Pallas kernels: 0 us -> 45.3 us
  matrix products: 27 us -> 0 us
  starting transfers between devices: 19.1 us -> 0 us
  blocking collectives: 16.5 us -> 0 us
  between operations: 14.4 us -> 0.83 us
  other arithmetic: 5.7 us -> 0 us
    all_gather x2 -> x0, waiting for transfers between devices: 110 us -> none  [the longest x1 84.6 us: per_device(): all_right = lax.all_gather(right_edge, 'dap', axis=1, tiled=True)]
    pallas_call x0 -> x1, Pallas kernels: none -> 45.3 us  [per_device(): pl.pallas_call(kernel, out_shape=(out, out), in_specs=[vmem, smem] + [vme...]
    dot_general x9 -> x0, matrix products: 27 us -> none  [the longest x1 8.04 us: per_device(): jnp.einsum('cik,cjk->cij', left_edge, all_right, preferred_element_type=j...]
    all_to_all x3 -> x0, starting transfers between devices: 19 us -> none  [the longest x1 12.1 us: per_device(): lax.all_to_all(grad_tri, 'dap', split_axis=2, concat_axis=1, tiled=True)]
    all_to_all x3 -> x0, blocking collectives: 16.5 us -> none  [copy_for_each(): return lax.all_to_all(copies, axis, split_axis=0, concat_axis=0, tiled=True)]
    all_to_all x3 -> x0, waiting for transfers between devices: 11.5 us -> none  [the longest x2 9.42 us: sum_at_owner(): lax.all_to_all(tiles, axis, split_axis=0, concat_axis=0, tiled=True)]
    unnamed x25 -> x27, local copies, waits for them, and re-layouts: 1.11 us -> 3.37 us
    reduce_sum x6 -> x0, other arithmetic: 2.14 us -> none  [the longest x1 1.28 us: layer_stats(): mean = jnp.mean(values, axis=-1, keepdims=True)]
  transfers between devices with their start and end apart: 5 -> 0, of which waited for: 5 -> 0; matrix products, arithmetic and copies ran while one was open for 10% -> 0% of each run, Pallas kernels for 0% -> 0%
where the time goes in v1:
time: 49.7 us; the launch traced here: 49.5 us
  Pallas kernels  45.3 us (91%)
  local copies, waits for them, and re-layouts  3.37 us (7%)
  between operations  0.83 us (2%)
    pallas_call x1, Pallas kernels, per_device(): pl.pallas_call(kernel, out_shape=(out, out), in_specs=[vmem, smem] + [vme...  45.3 us
    unnamed x27, local copies, waits for them, and re-layouts  3.37 us

profile of v1, /device:TPU:1, one launch (start us, length us, event | category | flops | bytes accessed | tf_op | source)
XLA Modules:
  0.0 49.5 jit_solution(3628725453312267039)
XLA Ops:
  0.6 0.0 copy-start.1
  0.6 0.0 copy-start.2
  0.7 0.0 copy-start.3
  0.7 0.0 copy-start.4
  0.7 0.0 copy-start.5
  0.7 0.0 copy-start.6
  0.7 0.0 copy-start.7
  0.7 0.0 copy-start.8
  0.7 0.0 copy-start.9
  0.7 0.0 copy-start.10
  0.7 0.0 copy-start.11
  0.7 1.1 %copy.15.pw = bf16[4,128,64]{2,1,0:T(8,128)(2,1)S(1)} copy(bf16[4,128,64]{1,2,0:T(8,128)(2,1)} %param.17) | data formatting | bytes 131072 | tf_op args[4]
  1.8 0.0 copy-done.1
  1.8 0.0 copy-done.2
  1.8 0.0 copy-done.3
  1.9 0.0 copy-done.4
  1.9 0.0 copy-done.5
  1.9 0.0 copy-done.6
  1.9 0.0 copy-done.7
  1.9 0.0 copy-done.8
  1.9 0.0 copy-done.9
  1.9 0.0 copy-done.10
  1.9 0.0 copy-done.11
  1.9 0.0 copy-start
  1.9 0.9 %copy-done = bf16[4,256,128]{2,1,0:T(8,128)(2,1)S(1)} copy-done((bf16[4,256,128]{2,1,0:T(8,128)(2,1)S(1)}, bf16[4,256,128]{2,1,0:T(8,128)(2,1)}, u32[]{:S(2)}) %copy-start) | copy-done | bytes 262168
  2.9 45.3 %shard_map.140 = (bf16[4,128,128]{2,1,0:T(8,128)(2,1)S(1)}, bf16[4,128,128]{2,1,0:T(8,128)(2,1)S(1)}) custom-call(bf16[4,256,128]{2,1,0:T(8,128)(2,1)S(1)} %copy-done, s32[4]{0:T(128)S(1)} %copy-done.5, f32[1,128]{1,0:T(1,128)S(1)} %bitcast.6, f32[1,128]{1,0:T(1,128)S(1)} %bitcast.7, bf16[4,128,64]{2,1,0:T(8,128)(2,1)S(1)} %copy.15.pw, ...), custom_call_target="tpu_custom_call" | custom-call | tf_op jit(solution)/shard_map/pallas_call | solution.py:356
  48.2 0.7 %copy.18 = bf16[4,128,128]{2,1,0:T(8,128)(2,1)} copy(bf16[4,128,128]{2,1,0:T(8,128)(2,1)S(1)} %get-tuple-element.4) | data formatting | bytes 262144
  48.9 0.7 %copy.19 = bf16[4,128,128]{2,1,0:T(8,128)(2,1)} copy(bf16[4,128,128]{2,1,0:T(8,128)(2,1)S(1)} %get-tuple-element.5) | data formatting | bytes 262144
Async XLA Ops:
  0.6 1.2 %copy-start.1 = (bf16[4,128,128]{2,1,0:T(8,128)(2,1)S(1)}, bf16[4,128,128]{2,1,0:T(8,128)(2,1)}, u32[]{:S(2)}) copy-start(bf16[4,128,128]{2,1,0:T(8,128)(2,1)} %cot.1) | copy-start | bytes 393220
  0.6 1.2 %copy-start.2 = (bf16[128,128]{1,0:T(8,128)(2,1)S(1)}, bf16[128,128]{1,0:T(8,128)(2,1)}, u32[]{:S(2)}) copy-start(bf16[128,128]{1,0:T(8,128)(2,1)} %w_gate.1) | copy-start | bytes 98308
  0.7 1.2 %copy-start.3 = (bf16[64,128]{1,0:T(8,128)(2,1)S(1)}, bf16[64,128]{1,0:T(8,128)(2,1)}, u32[]{:S(2)}) copy-start(bf16[64,128]{1,0:T(8,128)(2,1)} %w_out.1) | copy-start | bytes 49156
  0.7 1.2 %copy-start.4 = (f32[4,64]{1,0:T(4,128)S(1)}, f32[4,64]{1,0:T(4,128)}, u32[]{:S(2)}) copy-start(f32[4,64]{1,0:T(4,128)} %pb.1) | copy-start | bytes 3076
  0.7 1.2 %copy-start.5 = (s32[4]{0:T(128)S(1)}, s32[4]{0:T(128)}, u32[]{:S(2)}) copy-start(s32[4]{0:T(128)} %lens.1) | copy-start | bytes 52
  0.7 1.2 %copy-start.6 = (f32[128]{0:T(128)S(1)}, f32[128]{0:T(128)}, u32[]{:S(2)}) copy-start(f32[128]{0:T(128)} %param.15) | copy-start | bytes 1540
  0.7 1.2 %copy-start.7 = (f32[128]{0:T(128)S(1)}, f32[128]{0:T(128)}, u32[]{:S(2)}) copy-start(f32[128]{0:T(128)} %param.16) | copy-start | bytes 1540
  0.7 1.2 %copy-start.8 = (f32[64]{0:T(128)S(1)}, f32[64]{0:T(128)}, u32[]{:S(2)}) copy-start(f32[64]{0:T(128)} %param.19) | copy-start | bytes 772
  0.7 1.2 %copy-start.9 = (f32[64]{0:T(128)S(1)}, f32[64]{0:T(128)}, u32[]{:S(2)}) copy-start(f32[64]{0:T(128)} %param.20) | copy-start | bytes 772
  0.7 1.2 %copy-start.10 = (f32[128]{0:T(128)S(1)}, f32[128]{0:T(128)}, u32[]{:S(2)}) copy-start(f32[128]{0:T(128)} %param.22) | copy-start | bytes 1540
  0.7 1.2 %copy-start.11 = (f32[128]{0:T(128)S(1)}, f32[128]{0:T(128)}, u32[]{:S(2)}) copy-start(f32[128]{0:T(128)} %param.24) | copy-start | bytes 1540
  1.9 1.0 %copy-start = (bf16[4,256,128]{2,1,0:T(8,128)(2,1)S(1)}, bf16[4,256,128]{2,1,0:T(8,128)(2,1)}, u32[]{:S(2)}) copy-start(bf16[4,256,128]{2,1,0:T(8,128)(2,1)} %pair.1) | copy-start | bytes 786436

commit v2 on v1

--- a/solution.py
+++ b/solution.py
@@ -35,25 +35,46 @@
     return jnp.sum(x, axis=0, keepdims=True) * (1.0 / 128.0)
 
 
+def hops(n):
+    return (0, 1, 2, 1)[n]
+
+
+STEPS = sorted(
+    (
+        (dz, dy, dx, dc)
+        for dz in range(4)
+        for dy in range(4)
+        for dx in range(4)
+        for dc in range(2)
+        if dz + dy + dx + dc
+    ),
+    key=lambda s: (-hops(s[0]) - hops(s[1]) - hops(s[2]), (s[0] * 5 + s[1] * 3 + s[2]) % 4),
+)
+
+
 def kernel(
-    pair,
+    pair_in,
     lens,
-    ln_gain,
-    ln_bias,
-    pw,
-    pb,
-    out_gain,
-    out_bias,
-    w_out,
-    out_shift,
-    w_gate,
-    gate_bias,
-    cot,
+    ln_gain_in,
+    ln_bias_in,
+    pw_in,
+    pb_in,
+    out_gain_in,
+    out_bias_in,
+    w_out_in,
+    out_shift_in,
+    w_gate_in,
+    gate_bias_in,
+    cot_in,
     update,
     pair_grad,
+    pair,
+    cot,
+    w_gate,
     wt,
     wo,
     hv,
+    half,
     vec,
     pnorm,
     pscale,
@@ -66,6 +87,7 @@
     rmat,
     s2,
     r2,
+    s3f,
     s3,
     r3,
     gmat,
@@ -87,34 +109,55 @@
     wsem_r,
     ssem,
     rsem,
+    isem,
 ):
     p = lax.axis_index("dap")
     g = lax.axis_index("ch")
     me = g * 64 + p
 
+    z, y, x, core = p // 16, p // 4 % 4, p // 2 % 2 * 2 + g, p % 2
+    at_z = [(z + n) % 4 * 16 for n in range(4)]
+    at_y = [(y + n) % 4 * 4 for n in range(4)]
+    at_x = [(x + n) % 4 for n in range(4)]
+    at_zy = [[zn + yn for yn in at_y] for zn in at_z]
+    at_xc = [[xn // 2 * 2 + c for c in (core, 1 - core)] for xn in at_x]
+    at_g = [xn % 2 for xn in at_x]
+
+    def place(step):
+        dz, dy, dx, dc = step
+        return at_zy[dz][dy] + at_xc[dx][dc], at_g[dx]
+
     barrier = pltpu.get_barrier_semaphore()
-
-    def greet(k, carry):
-        t = lax.rem(me + k, 128)
+    loads = [
+        pltpu.make_async_copy(source, target, isem.at[n])
+        for n, (source, target) in enumerate(
+            (
+                (pair_in, pair),
+                (pw_in, wt.at[g]),
+                (ln_gain_in, vec.at[0:1]),
+                (ln_bias_in, vec.at[1:2]),
+                (out_shift_in, vec.at[2:3]),
+                (gate_bias_in, vec.at[3:4]),
+                (pb_in, half.at[0:4]),
+                (out_gain_in, half.at[4:5]),
+                (out_bias_in, half.at[5:6]),
+                (w_out_in, wo.at[g]),
+                (w_gate_in, w_gate),
+                (cot_in, cot),
+            )
+        )
+    ]
+    for load in loads:
+        load.start()
+    for step in STEPS:
         pl.semaphore_signal(
-            barrier, inc=1, device_id=(lax.rem(t, 64), t // 64), device_id_type=MESH
+            barrier, inc=1, device_id=place(step), device_id_type=MESH
         )
-        return carry
-
-    lax.fori_loop(1, 128, greet, 0)
-
-    for m in range(4):
-        wt[g, m * 64 : (m + 1) * 64, :] = pw[m].T
-    wo[g] = w_out[...]
+    for load in loads:
+        load.wait()
+
     hv[g] = jnp.zeros((8, 128), F32)
-    hv[g, 0:4, 0:64] = pb[...]
-    hv[g, 4:5, 0:64] = out_gain[...]
-    hv[g, 5:6, 0:64] = out_bias[...]
-    vec[...] = jnp.zeros((8, 128), F32)
-    vec[0:1, :] = ln_gain[...]
-    vec[1:2, :] = ln_bias[...]
-    vec[2:3, :] = out_shift[...]
-    vec[3:4, :] = gate_bias[...]
+    hv[g, 0:6, 0:64] = half[0:6]
     vcol = vec[...].T
     gain_c = column(vcol, 0, 128)
     bias_c = column(vcol, 1, 128)
@@ -154,24 +197,28 @@
             s1f[pl.ds(i * 4 + 2 + kh, 64, stride=16), :] = right
     s1[...] = s1f[...].reshape(64, 16, 128).astype(BF16)
 
+    gate_w = w_gate[...].T
+    gate_c = column(vcol, 3, 128)
+    own_columns = present_columns(g * 2)
+    for i in range(4):
+        gate = sigmoid(mm(gate_w, normed[i * 2 + g]) + gate_c)
+        gate_t[i] = gate
+        cot_t[i] = cot[i].T.astype(F32)
+
     pl.semaphore_wait(barrier, 127)
 
-    own1 = pltpu.make_async_copy(s1.at[p], r1.at[p], rsem.at[0])
-    own1.start()
-
-    def send1(k, carry):
-        t = lax.rem(p + k, 64)
-        pltpu.make_async_remote_copy(
-            src_ref=s1.at[t],
-            dst_ref=r1.at[p],
-            send_sem=ssem.at[0],
-            recv_sem=rsem.at[0],
-            device_id=(t, g),
-            device_id_type=MESH,
-        ).start()
-        return carry
-
-    lax.fori_loop(1, 64, send1, 0)
+    pltpu.make_async_copy(s1.at[p], r1.at[p], rsem.at[0]).start()
+    for step in STEPS:
+        if step[2] % 2 == 0:
+            t, _ = place(step)
+            pltpu.make_async_remote_copy(
+                src_ref=s1.at[t],
+                dst_ref=r1.at[p],
+                send_sem=ssem.at[0],
+                recv_sem=rsem.at[0],
+                device_id=(t, g),
+                device_id_type=MESH,
+            ).start()
 
     swaps = [
         pltpu.make_async_remote_copy(
@@ -187,13 +234,6 @@
     for swap in swaps:
         swap.start()
 
-    gate_w = w_gate[...].T
-    gate_c = column(vcol, 3, 128)
-    own_columns = present_columns(g * 2)
-    for i in range(4):
-        gate = sigmoid(mm(gate_w, normed[i * 2 + g]) + gate_c)
-        gate_t[i] = gate
-        cot_t[i] = cot[i].T.astype(F32)
     for swap in swaps:
         swap.wait()
     halves = [hv[0].T, hv[1].T]
@@ -235,25 +275,26 @@
             lmat[...], rmat[h * 128 : (h + 1) * 128, :]
         )
 
-    def spread(source, target, n):
-        mine = pl.ds(pl.multiple_of(me * 4, 4), 4)
-        pltpu.make_async_copy(source.at[mine], target.at[mine], rsem.at[n]).start()
-
-        def send(k, carry):
-            t = lax.rem(me + k, 128)
+    def spread(source, target, n, rows):
+        def block(ref, t):
+            if rows:
+                return ref.at[pl.ds(pl.multiple_of(t * rows, rows), rows)]
+            return ref.at[t]
+
+        mine = block(target, me)
+        pltpu.make_async_copy(block(source, me), mine, rsem.at[n]).start()
+        for step in STEPS:
+            t, tg = place(step)
             pltpu.make_async_remote_copy(
-                src_ref=source.at[pl.ds(pl.multiple_of(t * 4, 4), 4)],
-                dst_ref=target.at[mine],
+                src_ref=block(source, tg * 64 + t),
+                dst_ref=mine,
                 send_sem=ssem.at[n],
                 recv_sem=rsem.at[n],
-                device_id=(lax.rem(t, 64), t // 64),
+                device_id=(t, tg),
                 device_id_type=MESH,
             ).start()
-            return carry
-
-        lax.fori_loop(1, 128, send, 0)
-
-    spread(s2, r2, 1)
+
+    spread(s2, r2, 1, 4)
     pltpu.make_async_copy(r2, r2, rsem.at[1]).wait()
 
     for i in range(4):
@@ -264,8 +305,9 @@
         tn_t[i] = tn
         gs = gs_t[i]
         grad = scale * (gs - m1_t[i] - tn * mean0(gs * tn))
-        s3[pl.ds(i, 128, stride=4), :] = grad
-    spread(s3, r3, 2)
+        s3f[pl.ds(i, 128, stride=4), :] = grad
+    s3[...] = s3f[...].reshape(128, 4, 128).astype(BF16)
+    spread(s3, r3, 2, 0)
 
     shift_c = column(vcol, 2, 128)
     for i in range(4):
@@ -279,7 +321,8 @@
 
     pltpu.make_async_copy(r3, r3, rsem.at[2]).wait()
     for h in range(2):
-        gmat[:, h * 128 : (h + 1) * 128] = r3[h * 256 : (h + 1) * 256, :].astype(BF16)
+        part = r3[h * 64 : (h + 1) * 64].astype(F32).reshape(256, 128)
+        gmat[:, h * 128 : (h + 1) * 128] = part.astype(BF16)
     grads = (mm(gmat[...], rmat[...]), mm_tn(gmat[...], lmat[...]))
     for side in range(2):
         for h in range(2):
@@ -287,21 +330,7 @@
                 :, h * 128 : (h + 1) * 128
             ]
     s4[...] = s4f[...].reshape(128, 8, 128).astype(BF16)
-    pltpu.make_async_copy(s4.at[me], r4.at[me], rsem.at[3]).start()
-
-    def send4(k, carry):
-        t = lax.rem(me + k, 128)
-        pltpu.make_async_remote_copy(
-            src_ref=s4.at[t],
-            dst_ref=r4.at[me],
-            send_sem=ssem.at[3],
-            recv_sem=rsem.at[3],
-            device_id=(lax.rem(t, 64), t // 64),
-            device_id_type=MESH,
-        ).start()
-        return carry
-
-    lax.fori_loop(1, 128, send4, 0)
+    spread(s4, r4, 3, 0)
     pltpu.make_async_copy(r4, r4, rsem.at[3]).wait()
 
     r4f[...] = r4[...].astype(F32).reshape(1024, 128)
@@ -325,11 +354,11 @@
 
     blocks = s1.at[pl.ds(0, 63)]
     pltpu.make_async_copy(blocks, blocks, ssem.at[0]).wait()
-    for n, ref in ((1, s2), (2, s3)):
-        blocks = ref.at[pl.ds(0, 508)]
+    blocks = s2.at[pl.ds(0, 508)]
+    pltpu.make_async_copy(blocks, blocks, ssem.at[1]).wait()
+    for n, ref in ((2, s3), (3, s4)):
+        blocks = ref.at[pl.ds(0, 127)]
         pltpu.make_async_copy(blocks, blocks, ssem.at[n]).wait()
-    blocks = s4.at[pl.ds(0, 127)]
-    pltpu.make_async_copy(blocks, blocks, ssem.at[3]).wait()
 
 
 def per_device(
@@ -351,17 +380,22 @@
         return v.reshape(1, -1)
 
     vmem = pl.BlockSpec(memory_space=pltpu.VMEM)
+    hbm = pl.BlockSpec(memory_space=pltpu.HBM)
     smem = pl.BlockSpec(memory_space=pltpu.SMEM)
     out = jax.ShapeDtypeStruct((4, 128, 128), BF16)
     return pl.pallas_call(
         kernel,
         out_shape=(out, out),
-        in_specs=[vmem, smem] + [vmem] * 11,
+        in_specs=[hbm, smem] + [hbm] * 11,
         out_specs=(vmem, vmem),
         scratch_shapes=[
+            pltpu.VMEM((4, 256, 128), BF16),
+            pltpu.VMEM((4, 128, 128), BF16),
+            pltpu.VMEM((128, 128), BF16),
             pltpu.VMEM((2, 256, 128), BF16),
             pltpu.VMEM((2, 64, 128), BF16),
             pltpu.VMEM((2, 8, 128), F32),
+            pltpu.VMEM((8, 64), F32),
             pltpu.VMEM((8, 128), F32),
             pltpu.VMEM((8, 128, 128), F32),
             pltpu.VMEM((8, 1, 128), F32),
@@ -375,7 +409,8 @@
             pltpu.VMEM((512, 128), F32),
             pltpu.VMEM((512, 128), F32),
             pltpu.VMEM((512, 128), F32),
-            pltpu.VMEM((512, 128), F32),
+            pltpu.VMEM((128, 4, 128), BF16),
+            pltpu.VMEM((128, 4, 128), BF16),
             pltpu.VMEM((256, 256), BF16),
             pltpu.VMEM((1024, 128), F32),
             pltpu.VMEM((128, 8, 128), BF16),
@@ -395,16 +430,17 @@
             pltpu.SemaphoreType.DMA((3,)),
             pltpu.SemaphoreType.DMA((4,)),
             pltpu.SemaphoreType.DMA((4,)),
+            pltpu.SemaphoreType.DMA((12,)),
         ],
         compiler_params=pltpu.CompilerParams(
-            collective_id=0, has_side_effects=True, vmem_limit_bytes=40 << 20
+            collective_id=0, has_side_effects=True, vmem_limit_bytes=63 << 20
         ),
     )(
         pair,
         chain_lengths,
         row(ln_gain),
         row(ln_bias),
-        proj_weight,
+        jnp.swapaxes(proj_weight, 1, 2).reshape(256, 128),
         proj_bias,
         row(out_gain),
         row(out_bias),

time: 49.7 us -> 42.8 us (0.86)
  Pallas kernels: 45.3 us -> 39.7 us
  local copies, waits for them, and re-layouts: 3.37 us -> 2.26 us
    pallas_call x1, Pallas kernels: 45.3 us -> 39.7 us  [per_device(): pl.pallas_call(kernel, out_shape=(out, out), in_specs=[hbm, smem] + [hbm]...]
    unnamed x27 -> x4, local copies, waits for them, and re-layouts: 3.37 us -> 2.26 us
where the time goes in v2:
time: 42.8 us; the launch traced here: 42.6 us
  Pallas kernels  39.7 us (93%)
  local copies, waits for them, and re-layouts  2.26 us (5%)
  between operations  0.65 us (2%)
    pallas_call x1, Pallas kernels, per_device(): pl.pallas_call(kernel, out_shape=(out, out), in_specs=[hbm, smem] + [hbm]...  39.7 us
    unnamed x4, local copies, waits for them, and re-layouts  2.26 us

profile of v2, /device:TPU:1, one launch (start us, length us, event | category | flops | bytes accessed | tf_op | source)
XLA Modules:
  0.0 42.6 jit_solution(14160627291481750181)
XLA Ops:
  0.6 39.7 %shard_map.140 = (bf16[4,128,128]{2,1,0:T(8,128)(2,1)}, bf16[4,128,128]{2,1,0:T(8,128)(2,1)}) custom-call(bf16[4,256,128]{2,1,0:T(8,128)(2,1)} %pair_in.1, s32[4]{0:T(128)} %lens.1, f32[1,128]{1,0:T(1,128)} %bitcast.10, f32[1,128]{1,0:T(1,128)} %bitcast.11, bf16[256,128]{1,0:T(8,128)(2,1)} %bitcast.9, f32[4,64]{1,0:T(4,128)} %pb_in.1, f32[1,64]{1,0:T(1,128)} %bitcast.12, ...), custom_call_target="tpu_custom_call" | custom-call | tf_op jit(solution)/shard_map/pallas_call | solution.py:386
  40.4 0.0 copy-start
  40.4 1.6 %copy.17 = bf16[4,128,128]{2,1,0:T(8,128)(2,1)} copy(bf16[4,128,128]{2,1,0:T(8,128)(2,1)} %get-tuple-element.4) | data formatting | bytes 262144
  42.0 0.0 copy-done
  42.0 0.7 %copy.18 = bf16[4,128,128]{2,1,0:T(8,128)(2,1)} copy(bf16[4,128,128]{2,1,0:T(8,128)(2,1)S(1)} %copy-done) | data formatting | bytes 262144
Async XLA Ops:
  40.4 1.6 %copy-start = (bf16[4,128,128]{2,1,0:T(8,128)(2,1)S(1)}, bf16[4,128,128]{2,1,0:T(8,128)(2,1)}, u32[]{:S(2)}) copy-start(bf16[4,128,128]{2,1,0:T(8,128)(2,1)} %get-tuple-element.5) | copy-start | bytes 393220

commit v3 on v2

--- a/solution.py
+++ b/solution.py
@@ -66,8 +66,7 @@
     w_gate_in,
     gate_bias_in,
     cot_in,
-    update,
-    pair_grad,
+    outs,
     pair,
     cot,
     w_gate,
@@ -128,6 +127,10 @@
         return at_zy[dz][dy] + at_xc[dx][dc], at_g[dx]
 
     barrier = pltpu.get_barrier_semaphore()
+    for step in STEPS:
+        pl.semaphore_signal(
+            barrier, inc=1, device_id=place(step), device_id_type=MESH
+        )
     loads = [
         pltpu.make_async_copy(source, target, isem.at[n])
         for n, (source, target) in enumerate(
@@ -149,10 +152,6 @@
     ]
     for load in loads:
         load.start()
-    for step in STEPS:
-        pl.semaphore_signal(
-            barrier, inc=1, device_id=place(step), device_id_type=MESH
-        )
     for load in loads:
         load.wait()
 
@@ -315,7 +314,7 @@
         out_sum = mm(wo_t[...], tri_out) + shift_c
         gate = gate_t[i]
         gated = gate * out_sum
-        update[i] = gated.T.astype(BF16)
+        outs[0, i] = gated.T.astype(BF16)
         grad_gate = (cot_t[i] * gated * (1.0 - gate)).astype(BF16)
         part_t[i] = mm(w_gate[...], grad_gate)
 
@@ -350,7 +349,7 @@
         ps = grad * gain_c
         norm = pnorm[i * 2 + g]
         own = pscale[i * 2 + g] * (ps - mean0(ps) - norm * mean0(ps * norm))
-        pair_grad[i] = own.T.astype(BF16)
+        outs[1, i] = own.T.astype(BF16)
 
     blocks = s1.at[pl.ds(0, 63)]
     pltpu.make_async_copy(blocks, blocks, ssem.at[0]).wait()
@@ -359,6 +358,17 @@
     for n, ref in ((2, s3), (3, s4)):
         blocks = ref.at[pl.ds(0, 127)]
         pltpu.make_async_copy(blocks, blocks, ssem.at[n]).wait()
+
+
+def publish(outs, update, pair_grad, sem):
+    copies = [
+        pltpu.make_async_copy(outs.at[n], target, sem.at[n])
+        for n, target in enumerate((update, pair_grad))
+    ]
+    for copy in copies:
+        copy.start()
+    for copy in copies:
+        copy.wait()
 
 
 def per_device(
@@ -383,11 +393,11 @@
     hbm = pl.BlockSpec(memory_space=pltpu.HBM)
     smem = pl.BlockSpec(memory_space=pltpu.SMEM)
     out = jax.ShapeDtypeStruct((4, 128, 128), BF16)
-    return pl.pallas_call(
+    outs = pl.pallas_call(
         kernel,
-        out_shape=(out, out),
+        out_shape=jax.ShapeDtypeStruct((2, 4, 128, 128), BF16),
         in_specs=[hbm, smem] + [hbm] * 11,
-        out_specs=(vmem, vmem),
+        out_specs=vmem,
         scratch_shapes=[
             pltpu.VMEM((4, 256, 128), BF16),
             pltpu.VMEM((4, 128, 128), BF16),
@@ -450,6 +460,13 @@
         row(gate_bias),
         cotangent,
     )
+    return pl.pallas_call(
+        publish,
+        out_shape=(out, out),
+        in_specs=[vmem],
+        out_specs=(hbm, hbm),
+        scratch_shapes=[pltpu.SemaphoreType.DMA((2,))],
+    )(outs)
 
 
 def solution(mesh):

time: 42.8 us -> 42.2 us (0.986)
  local copies, waits for them, and re-layouts: 2.26 us -> 0 us
  Pallas kernels: 39.7 us -> 41.3 us
    unnamed x4 -> x0, local copies, waits for them, and re-layouts: 2.26 us -> none
    pallas_call x1 -> x2, Pallas kernels: 39.7 us -> 41.3 us  [the longest x1 39.7 us: per_device(): pl.pallas_call(kernel, out_shape=jax.ShapeDtypeStruct((2, 4, 128, 128), B...]
where the time goes in v3:
time: 42.2 us; the launch traced here: 42 us
  Pallas kernels  41.3 us (98%)
  between operations  0.64 us (2%)
    pallas_call x1, Pallas kernels, per_device(): pl.pallas_call(kernel, out_shape=jax.ShapeDtypeStruct((2, 4, 128, 128), B...  39.7 us
    pallas_call x1, Pallas kernels, per_device(): pl.pallas_call(publish, out_shape=(out, out), in_specs=[vmem], out_specs=...  1.66 us

profile of v3, /device:TPU:1, one launch (start us, length us, event | category | flops | bytes accessed | tf_op | source)
XLA Modules:
  0.0 42.0 jit_solution(6455939382232594951)
XLA Ops:
  0.6 39.7 %shard_map.140.outs = bf16[2,4,128,128]{3,2,1,0:T(8,128)(2,1)} custom-call(bf16[4,256,128]{2,1,0:T(8,128)(2,1)} %pair_in.1, s32[4]{0:T(128)} %lens.1, f32[1,128]{1,0:T(1,128)} %bitcast.10, f32[1,128]{1,0:T(1,128)} %bitcast.11, bf16[256,128]{1,0:T(8,128)(2,1)} %bitcast.9, f32[4,64]{1,0:T(4,128)} %pb_in.1, f32[1,64]{1,0:T(1,128)} %bitcast.12, ...), custom_call_target="tpu_custom_call" | custom-call | tf_op jit(solution)/shard_map/pallas_call | solution.py:396
  40.3 1.7 %shard_map.141 = (bf16[4,128,128]{2,1,0:T(8,128)(2,1)}, bf16[4,128,128]{2,1,0:T(8,128)(2,1)}) custom-call(bf16[2,4,128,128]{3,2,1,0:T(8,128)(2,1)} %shard_map.140.outs), custom_call_target="tpu_custom_call" | custom-call | tf_op jit(solution)/shard_map/pallas_call | solution.py:463

commit v4 on v3

--- a/solution.py
+++ b/solution.py
@@ -1,3 +1,5 @@
+import random
+
 import jax
 import jax.numpy as jnp
 from jax import lax
@@ -39,17 +41,16 @@
     return (0, 1, 2, 1)[n]
 
 
-STEPS = sorted(
-    (
-        (dz, dy, dx, dc)
-        for dz in range(4)
-        for dy in range(4)
-        for dx in range(4)
-        for dc in range(2)
-        if dz + dy + dx + dc
-    ),
-    key=lambda s: (-hops(s[0]) - hops(s[1]) - hops(s[2]), (s[0] * 5 + s[1] * 3 + s[2]) % 4),
-)
+STEPS = [
+    (dz, dy, dx, dc)
+    for dz in range(4)
+    for dy in range(4)
+    for dx in range(4)
+    for dc in range(2)
+    if dz + dy + dx + dc
+]
+random.Random(1).shuffle(STEPS)
+STEPS.sort(key=lambda s: -hops(s[0]) - hops(s[1]) - hops(s[2]))
 
 
 def kernel(

time: 42.2 us -> 41.5 us (0.983)
  Pallas kernels: 41.3 us -> 40.7 us
    pallas_call x1, Pallas kernels: 39.7 us -> 39.1 us  [per_device(): pl.pallas_call(kernel, out_shape=jax.ShapeDtypeStruct((2, 4, 128, 128), B...]
where the time goes in v4:
time: 41.5 us; the launch traced here: 41.4 us
  Pallas kernels  40.7 us (98%)
  between operations  0.64 us (2%)
    pallas_call x1, Pallas kernels, per_device(): pl.pallas_call(kernel, out_shape=jax.ShapeDtypeStruct((2, 4, 128, 128), B...  39.1 us
    pallas_call x1, Pallas kernels, per_device(): pl.pallas_call(publish, out_shape=(out, out), in_specs=[vmem], out_specs=...  1.66 us

profile of v4, /device:TPU:1, one launch (start us, length us, event | category | flops | bytes accessed | tf_op | source)
XLA Modules:
  0.0 41.4 jit_solution(571218574670157630)
XLA Ops:
  0.6 39.1 %shard_map.140.outs = bf16[2,4,128,128]{3,2,1,0:T(8,128)(2,1)} custom-call(bf16[4,256,128]{2,1,0:T(8,128)(2,1)} %pair_in.1, s32[4]{0:T(128)} %lens.1, f32[1,128]{1,0:T(1,128)} %bitcast.10, f32[1,128]{1,0:T(1,128)} %bitcast.11, bf16[256,128]{1,0:T(8,128)(2,1)} %bitcast.9, f32[4,64]{1,0:T(4,128)} %pb_in.1, f32[1,64]{1,0:T(1,128)} %bitcast.12, ...), custom_call_target="tpu_custom_call" | custom-call | tf_op jit(solution)/shard_map/pallas_call | solution.py:397
  39.7 1.7 %shard_map.141 = (bf16[4,128,128]{2,1,0:T(8,128)(2,1)}, bf16[4,128,128]{2,1,0:T(8,128)(2,1)}) custom-call(bf16[2,4,128,128]{3,2,1,0:T(8,128)(2,1)} %shard_map.140.outs), custom_call_target="tpu_custom_call" | custom-call | tf_op jit(solution)/shard_map/pallas_call | solution.py:464

commit v5 on v4

--- a/solution.py
+++ b/solution.py
@@ -49,7 +49,7 @@
     for dc in range(2)
     if dz + dy + dx + dc
 ]
-random.Random(1).shuffle(STEPS)
+random.Random(4).shuffle(STEPS)
 STEPS.sort(key=lambda s: -hops(s[0]) - hops(s[1]) - hops(s[2]))
 
 
@@ -91,7 +91,6 @@
     s3,
     r3,
     gmat,
-    s4f,
     s4,
     r4,
     r4f,
@@ -116,9 +115,12 @@
     me = g * 64 + p
 
     z, y, x, core = p // 16, p // 4 % 4, p // 2 % 2 * 2 + g, p % 2
-    at_z = [(z + n) % 4 * 16 for n in range(4)]
-    at_y = [(y + n) % 4 * 4 for n in range(4)]
-    at_x = [(x + n) % 4 for n in range(4)]
+    turn_z, turn_y, turn_x = (
+        1 + 2 * ((n + core) % 2) for n in (x + y, x + z, y + z)
+    )
+    at_z = [(z + n * turn_z) % 4 * 16 for n in range(4)]
+    at_y = [(y + n * turn_y) % 4 * 4 for n in range(4)]
+    at_x = [(x + n * turn_x) % 4 for n in range(4)]
     at_zy = [[zn + yn for yn in at_y] for zn in at_z]
     at_xc = [[xn // 2 * 2 + c for c in (core, 1 - core)] for xn in at_x]
     at_g = [xn % 2 for xn in at_x]
@@ -324,19 +326,17 @@
         part = r3[h * 64 : (h + 1) * 64].astype(F32).reshape(256, 128)
         gmat[:, h * 128 : (h + 1) * 128] = part.astype(BF16)
     grads = (mm(gmat[...], rmat[...]), mm_tn(gmat[...], lmat[...]))
-    for side in range(2):
-        for h in range(2):
-            s4f[pl.ds(h * 512 + side, 256, stride=2), :] = grads[side][
-                :, h * 128 : (h + 1) * 128
-            ]
-    s4[...] = s4f[...].reshape(128, 8, 128).astype(BF16)
+    for h in range(2):
+        cols = slice(h * 128, (h + 1) * 128)
+        pieces = [grad[:, cols].reshape(64, 4, 128) for grad in grads]
+        s4[h * 64 : (h + 1) * 64] = jnp.concatenate(pieces, axis=1).astype(BF16)
     spread(s4, r4, 3, 0)
     pltpu.make_async_copy(r4, r4, rsem.at[3]).wait()
 
     r4f[...] = r4[...].astype(F32).reshape(1024, 128)
     for i in range(4):
         for side in range(2):
-            edge = r4f[pl.ds(i * 2 + side, 128, stride=8), :]
+            edge = r4f[pl.ds(side * 4 + i, 128, stride=8), :]
             for n in range(2):
                 m = side * 2 + n
                 prod = (edge * factor[i, m]).astype(BF16)
@@ -423,7 +423,6 @@
             pltpu.VMEM((128, 4, 128), BF16),
             pltpu.VMEM((128, 4, 128), BF16),
             pltpu.VMEM((256, 256), BF16),
-            pltpu.VMEM((1024, 128), F32),
             pltpu.VMEM((128, 8, 128), BF16),
             pltpu.VMEM((128, 8, 128), BF16),
             pltpu.VMEM((1024, 128), F32),

time: 41.5 us -> 41.4 us (level)
  no operation moved by 1% of the time
where the time goes in v5:
time: 41.4 us; the launch traced here: 41.2 us
  Pallas kernels  40.5 us (98%)
  between operations  0.64 us (2%)
    pallas_call x1, Pallas kernels, per_device(): pl.pallas_call(kernel, out_shape=jax.ShapeDtypeStruct((2, 4, 128, 128), B...  38.9 us
    pallas_call x1, Pallas kernels, per_device(): pl.pallas_call(publish, out_shape=(out, out), in_specs=[vmem], out_specs=...  1.66 us

profile of v5, /device:TPU:1, one launch (start us, length us, event | category | flops | bytes accessed | tf_op | source)
XLA Modules:
  0.0 41.2 jit_solution(3484165486677901829)
XLA Ops:
  0.6 38.9 %shard_map.140.outs = bf16[2,4,128,128]{3,2,1,0:T(8,128)(2,1)} custom-call(bf16[4,256,128]{2,1,0:T(8,128)(2,1)} %pair_in.1, s32[4]{0:T(128)} %lens.1, f32[1,128]{1,0:T(1,128)} %bitcast.10, f32[1,128]{1,0:T(1,128)} %bitcast.11, bf16[256,128]{1,0:T(8,128)(2,1)} %bitcast.9, f32[4,64]{1,0:T(4,128)} %pb_in.1, f32[1,64]{1,0:T(1,128)} %bitcast.12, ...), custom_call_target="tpu_custom_call" | custom-call | tf_op jit(solution)/shard_map/pallas_call | solution.py:397
  39.5 1.7 %shard_map.141 = (bf16[4,128,128]{2,1,0:T(8,128)(2,1)}, bf16[4,128,128]{2,1,0:T(8,128)(2,1)}) custom-call(bf16[2,4,128,128]{3,2,1,0:T(8,128)(2,1)} %shard_map.140.outs), custom_call_target="tpu_custom_call" | custom-call | tf_op jit(solution)/shard_map/pallas_call | solution.py:463

commit v6 on v4

--- a/solution.py
+++ b/solution.py
@@ -231,10 +231,10 @@
         )
         for n, ref in enumerate((wt, wo, hv))
     ]
-    for swap in swaps:
+    for swap in swaps[1:]:
         swap.start()
 
-    for swap in swaps:
+    for swap in swaps[1:]:
         swap.wait()
     halves = [hv[0].T, hv[1].T]
     full = [
@@ -248,6 +248,77 @@
         gs_t[i] = gs
         m1_t[i] = mean0(gs)
     wo_t[...] = wo_full.T
+
+    pltpu.make_async_copy(r1, r1, rsem.at[0]).wait()
+    r1f[...] = r1[...].reshape(1024, 128).astype(F32)
+    for kh in range(2):
+        cols = slice(kh * 128, (kh + 1) * 128)
+        lmat[:, cols] = r1f[pl.ds(kh, 256, stride=4), :].astype(BF16)
+        rmat[:, cols] = r1f[pl.ds(2 + kh, 256, stride=4), :].astype(BF16)
+    for h in range(2):
+        s2[h * 256 : (h + 1) * 256, :] = mm_nt(
+            lmat[...], rmat[h * 128 : (h + 1) * 128, :]
+        )
+
+    def spread(source, target, n, rows):
+        def block(ref, t):
+            if rows:
+                return ref.at[pl.ds(pl.multiple_of(t * rows, rows), rows)]
+            return ref.at[t]
+
+        mine = block(target, me)
+        pltpu.make_async_copy(block(source, me), mine, rsem.at[n]).start()
+        for step in STEPS:
+            t, tg = place(step)
+            pltpu.make_async_remote_copy(
+                src_ref=block(source, tg * 64 + t),
+                dst_ref=mine,
+                send_sem=ssem.at[n],
+                recv_sem=rsem.at[n],
+                device_id=(t, tg),
+                device_id_type=MESH,
+            ).start()
+
+    spread(s2, r2, 1, 4)
+    pltpu.make_async_copy(r2, r2, rsem.at[1]).wait()
+
+    for i in range(4):
+        tri = r2[pl.ds(i, 128, stride=4), :]
+        mean = mean0(tri)
+        scale = lax.rsqrt(mean0(tri * tri) - mean * mean + EPS)
+        tn = (tri - mean) * scale
+        tn_t[i] = tn
+        gs = gs_t[i]
+        grad = scale * (gs - m1_t[i] - tn * mean0(gs * tn))
+        s3f[pl.ds(i, 128, stride=4), :] = grad
+    s3[...] = s3f[...].reshape(128, 4, 128).astype(BF16)
+    spread(s3, r3, 2, 0)
+    swaps[0].start()
+
+    shift_c = column(vcol, 2, 128)
+    for i in range(4):
+        tri_out = (tn_t[i] * full[0] + full[1]).astype(BF16)
+        out_sum = mm(wo_t[...], tri_out) + shift_c
+        gate = gate_t[i]
+        gated = gate * out_sum
+        outs[0, i] = gated.T.astype(BF16)
+        grad_gate = (cot_t[i] * gated * (1.0 - gate)).astype(BF16)
+        part_t[i] = mm(w_gate[...], grad_gate)
+
+    pltpu.make_async_copy(r3, r3, rsem.at[2]).wait()
+    for h in range(2):
+        part = r3[h * 64 : (h + 1) * 64].astype(F32).reshape(256, 128)
+        gmat[:, h * 128 : (h + 1) * 128] = part.astype(BF16)
+    grads = (mm(gmat[...], rmat[...]), mm_tn(gmat[...], lmat[...]))
+    for side in range(2):
+        for h in range(2):
+            s4f[pl.ds(h * 512 + side, 256, stride=2), :] = grads[side][
+                :, h * 128 : (h + 1) * 128
+            ]
+    s4[...] = s4f[...].reshape(128, 8, 128).astype(BF16)
+    spread(s4, r4, 3, 0)
+
+    swaps[0].wait()
     back_w[...] = wt[...].reshape(512, 128).astype(F32).T.astype(BF16)
 
     for h in range(2):
@@ -264,73 +335,6 @@
                 factor[i, n, rows, :] = value * sm * (1.0 - s)
                 factor[i, n + 1, rows, :] = sm
 
-    pltpu.make_async_copy(r1, r1, rsem.at[0]).wait()
-    r1f[...] = r1[...].reshape(1024, 128).astype(F32)
-    for kh in range(2):
-        cols = slice(kh * 128, (kh + 1) * 128)
-        lmat[:, cols] = r1f[pl.ds(kh, 256, stride=4), :].astype(BF16)
-        rmat[:, cols] = r1f[pl.ds(2 + kh, 256, stride=4), :].astype(BF16)
-    for h in range(2):
-        s2[h * 256 : (h + 1) * 256, :] = mm_nt(
-            lmat[...], rmat[h * 128 : (h + 1) * 128, :]
-        )
-
-    def spread(source, target, n, rows):
-        def block(ref, t):
-            if rows:
-                return ref.at[pl.ds(pl.multiple_of(t * rows, rows), rows)]
-            return ref.at[t]
-
-        mine = block(target, me)
-        pltpu.make_async_copy(block(source, me), mine, rsem.at[n]).start()
-        for step in STEPS:
-            t, tg = place(step)
-            pltpu.make_async_remote_copy(
-                src_ref=block(source, tg * 64 + t),
-                dst_ref=mine,
-                send_sem=ssem.at[n],
-                recv_sem=rsem.at[n],
-                device_id=(t, tg),
-                device_id_type=MESH,
-            ).start()
-
-    spread(s2, r2, 1, 4)
-    pltpu.make_async_copy(r2, r2, rsem.at[1]).wait()
-
-    for i in range(4):
-        tri = r2[pl.ds(i, 128, stride=4), :]
-        mean = mean0(tri)
-        scale = lax.rsqrt(mean0(tri * tri) - mean * mean + EPS)
-        tn = (tri - mean) * scale
-        tn_t[i] = tn
-        gs = gs_t[i]
-        grad = scale * (gs - m1_t[i] - tn * mean0(gs * tn))
-        s3f[pl.ds(i, 128, stride=4), :] = grad
-    s3[...] = s3f[...].reshape(128, 4, 128).astype(BF16)
-    spread(s3, r3, 2, 0)
-
-    shift_c = column(vcol, 2, 128)
-    for i in range(4):
-        tri_out = (tn_t[i] * full[0] + full[1]).astype(BF16)
-        out_sum = mm(wo_t[...], tri_out) + shift_c
-        gate = gate_t[i]
-        gated = gate * out_sum
-        outs[0, i] = gated.T.astype(BF16)
-        grad_gate = (cot_t[i] * gated * (1.0 - gate)).astype(BF16)
-        part_t[i] = mm(w_gate[...], grad_gate)
-
-    pltpu.make_async_copy(r3, r3, rsem.at[2]).wait()
-    for h in range(2):
-        part = r3[h * 64 : (h + 1) * 64].astype(F32).reshape(256, 128)
-        gmat[:, h * 128 : (h + 1) * 128] = part.astype(BF16)
-    grads = (mm(gmat[...], rmat[...]), mm_tn(gmat[...], lmat[...]))
-    for side in range(2):
-        for h in range(2):
-            s4f[pl.ds(h * 512 + side, 256, stride=2), :] = grads[side][
-                :, h * 128 : (h + 1) * 128
-            ]
-    s4[...] = s4f[...].reshape(128, 8, 128).astype(BF16)
-    spread(s4, r4, 3, 0)
     pltpu.make_async_copy(r4, r4, rsem.at[3]).wait()
 
     r4f[...] = r4[...].astype(F32).reshape(1024, 128)

time: 41.5 us -> 41.4 us (level)
  no operation moved by 1% of the time
where the time goes in v6:
time: 41.4 us; the launch traced here: 41.2 us
  Pallas kernels  40.6 us (98%)
  between operations  0.64 us (2%)
    pallas_call x1, Pallas kernels, per_device(): pl.pallas_call(kernel, out_shape=jax.ShapeDtypeStruct((2, 4, 128, 128), B...  38.9 us
    pallas_call x1, Pallas kernels, per_device(): pl.pallas_call(publish, out_shape=(out, out), in_specs=[vmem], out_specs=...  1.66 us

profile of v6, /device:TPU:1, one launch (start us, length us, event | category | flops | bytes accessed | tf_op | source)
XLA Modules:
  0.0 41.2 jit_solution(11914785430092960376)
XLA Ops:
  0.6 38.9 %shard_map.140.outs = bf16[2,4,128,128]{3,2,1,0:T(8,128)(2,1)} custom-call(bf16[4,256,128]{2,1,0:T(8,128)(2,1)} %pair_in.1, s32[4]{0:T(128)} %lens.1, f32[1,128]{1,0:T(1,128)} %bitcast.10, f32[1,128]{1,0:T(1,128)} %bitcast.11, bf16[256,128]{1,0:T(8,128)(2,1)} %bitcast.9, f32[4,64]{1,0:T(4,128)} %pb_in.1, f32[1,64]{1,0:T(1,128)} %bitcast.12, ...), custom_call_target="tpu_custom_call" | custom-call | tf_op jit(solution)/shard_map/pallas_call | solution.py:401
  39.6 1.7 %shard_map.141 = (bf16[4,128,128]{2,1,0:T(8,128)(2,1)}, bf16[4,128,128]{2,1,0:T(8,128)(2,1)}) custom-call(bf16[2,4,128,128]{3,2,1,0:T(8,128)(2,1)} %shard_map.140.outs), custom_call_target="tpu_custom_call" | custom-call | tf_op jit(solution)/shard_map/pallas_call | solution.py:468
